TPU v7x, 32 devices: a whole 2x2x4 slice. The times are simulated.
32 devices in a mesh: dp: 8 (over y, x, core), mp: 4 (over z).
Axes of the slice: x: 2, y: 2, z: 4, core: 2. Of those that a mesh axis runs over, the one named last changes fastest.
Arguments:
- hidden_acts: bfloat16 [12288, 1024], P('dp'), may hold values from -3072 to 3072
- out_grads: bfloat16 [12288, 8192], P('dp', 'mp'), may hold values from -6 to 6
- token_counts: int32 [8], P('dp'), may hold values from 1 to 1536, as said below
- down_weight: bfloat16 [1024, 8192], P(None, 'mp'), may hold values from -0.0625 to 0.0625
- owner_map: int32 [8], replicated, may hold values from 0 to 7, each once
- master: float32 [1024, 8192], P('dp', 'mp'), may hold values from -0.046875 to 0.046875
- moment1: float32 [1024, 8192], P('dp', 'mp'), may hold values from -6 to 6
- moment2: bfloat16 [1024, 8192], P('dp', 'mp'), may hold values from 0.099609375 to 10
Outputs:
- master_new: float32 [1024, 8192], P('dp', 'mp')
- moment1_new: float32 [1024, 8192], P('dp', 'mp')
- moment2_new: bfloat16 [1024, 8192], P('dp', 'mp')
- weights_new: bfloat16 [1024, 8192], P(None, 'mp')
- input_grads: bfloat16 [12288, 1024], P('dp', 'mp')
Inputs may be any that keep to these rules, and one draw needn't show every extreme that they name: `token_counts`: the last worker is always full; the others hold from about a third to all of their 1536 slots, rising along the workers.
All inputs are finite; a program needn't handle non-finite values.
Results may differ from a plain program's by a relative error of at most 0.0026.
Values may be sent and summed in bfloat16 or wider, within the bound.
A program may use at most 128 MiB of HBM per device.

v0:
```python
import jax
import jax.numpy as jnp
from jax import lax
from jax.sharding import PartitionSpec as P

beta_one = 0.9
beta_two = 0.95
learn_rate = 0.0003
epsilon = 1e-08
correct_one = 1.0 - 0.9**50
correct_two = 1.0 - 0.95**50


def per_device(
    hidden_acts, out_grads, token_counts, down_weight, owner_map, master, moment1, moment2
):
    rows = out_grads.shape[0]
    columns = out_grads.shape[1]
    hidden = hidden_acts.shape[1]
    workers = lax.axis_size("dp")
    block = hidden // workers
    valid = lax.iota(jnp.int32, rows) < token_counts[0]
    masked = jnp.where(valid[:, None], out_grads, jnp.zeros_like(out_grads))
    total = lax.psum(token_counts, "dp")
    total = jnp.sum(total).astype(jnp.float32)
    partial_value = lax.dot_general(
        hidden_acts, masked, (((0,), (0,)), ((), ())), preferred_element_type=jnp.float32
    )
    slotted = jnp.take(
        partial_value.astype(jnp.bfloat16).reshape(workers, block, columns), owner_map, axis=0
    )
    received = lax.all_to_all(slotted, "dp", split_axis=0, concat_axis=0, tiled=True)
    summed = jnp.sum(received.astype(jnp.float32), axis=0)
    grad = summed / total
    moment1_new = beta_one * moment1 + (1.0 - beta_one) * grad
    second = beta_two * moment2.astype(jnp.float32) + (1.0 - beta_two) * grad * grad
    moment2_new = second.astype(jnp.bfloat16)
    master_new = master - learn_rate * (moment1_new / correct_one) / (
        jnp.sqrt(second / correct_two) + epsilon
    )
    gathered = lax.all_gather(master_new.astype(jnp.bfloat16), "dp", axis=0, tiled=True)
    inverse = jnp.zeros((workers,), jnp.int32).at[owner_map].set(lax.iota(jnp.int32, workers))
    weights_new = jnp.take(gathered.reshape(workers, block, columns), inverse, axis=0).reshape(
        hidden, columns
    )
    feature_part = lax.dot_general(
        masked, down_weight, (((1,), (1,)), ((), ())), preferred_element_type=jnp.float32
    )
    input_grads = lax.psum_scatter(feature_part, "mp", scatter_dimension=1, tiled=True).astype(
        jnp.bfloat16
    )
    return (master_new, moment1_new, moment2_new, weights_new, input_grads)


def solution(mesh):
    in_specs = (
        P("dp", None),
        P("dp", "mp"),
        P("dp"),
        P(None, "mp"),
        P(),
        P("dp", "mp"),
        P("dp", "mp"),
        P("dp", "mp"),
    )
    out_specs = (P("dp", "mp"), P("dp", "mp"), P("dp", "mp"), P(None, "mp"), P("dp", "mp"))
    return jax.shard_map(
        per_device, mesh=mesh, in_specs=in_specs, out_specs=out_specs, check_vma=False
    )
```

profile of v0, /device:TPU:16, one launch (start us, length us, event | category | flops | bytes accessed | tf_op | source)
XLA Modules:
  0.0 226.6 jit_solution(1295683149713437074)
XLA Ops:
  8.0 0.0 copy-start
  8.0 0.8 compare_select_fusion.1
  8.8 0.8 compare_and_fusion.1
  10.3 0.0 copy-done
  10.3 11.4 %convolution_convert_fusion = bf16[2048,1024]{0,1:T(8,128)(2,1)} fusion(bf16[1536,1024]{1,0:T(8,128)(2,1)S(1)} %copy-done, bf16[1536,2048]{1,0:T(8,128)(2,1)} %param.11, pred[1536]{0:T(1024)(128)(4,1)S(1)} %iota_compare_fusion), kind=kOutput, calls=%fused_computation.7 | convolution fusion | flops 6447693824 | bytes 13633024 | tf_op jit(solution)/shard_map/dot_general | solution.py:26
  21.7 4.9 %gather_fusion = bf16[8,128,2048]{2,1,0:T(8,128)(2,1)} fusion(bf16[8,128,2048]{2,1,0:T(8,128)(2,1)} %bitcast.13, s32[1024]{0:T(1024)S(1)} %pad_clamp_fusion.1), kind=kCustom, calls=%fused_computation.clone | custom fusion | bytes 8388640 | tf_op jit(solution)/shard_map/jit(_take)/gather | solution.py:29
  26.6 4.7 %broadcast_select_fusion.2 = bf16[8,128,2048]{2,1,0:T(8,128)(2,1)} fusion(bf16[8,128,2048]{2,1,0:T(8,128)(2,1)} %gather_fusion, pred[8]{0:T(512)(128)(4,1)S(1)} %compare_and_fusion.1), kind=kLoop, calls=%fused_computation.6 | loop fusion | flops 2097152 | bytes 8388616 | tf_op jit(solution)/shard_map/jit(_take)/select_n | solution.py:29
  31.3 4.5 %all-to-all-start = ((bf16[8,128,2048]{2,1,0:T(8,128)(2,1)}), bf16[8,128,2048]{2,1,0:T(8,128)(2,1)}, u32[]{:S(2)}, u32[]{:S(2)}) async-start(bf16[8,128,2048]{2,1,0:T(8,128)(2,1)} %broadcast_select_fusion.2), calls=%async_computation | async-start | bytes 8388608 | tf_op jit(solution)/shard_map/all_to_all | solution.py:32
  35.8 0.0 all-gather.2.cloned.1.call-start
  35.9 51.7 %psum.7 = s32[1]{0:T(128)} all-reduce(s32[1]{0:T(128)} %param.12), channel_id=1, replica_groups=mesh['dp'=8,'mp'=4] {'dp'}, use_global_device_ids=true, to_apply=%region_1.0 | all-reduce | flops 1 | bytes 8 | tf_op jit(solution)/shard_map/psum | solution.py:24
  88.3 0.0 all-to-all-done
  88.3 0.0 copy-start.1
  88.3 0.0 copy-start.2
  88.3 0.0 copy-start.3
  88.3 3.2 %convert_reduce_fusion = f32[128,2048]{1,0:T(8,128)S(1)} fusion(bf16[8,128,2048]{2,1,0:T(8,128)(2,1)} %all-to-all-done), kind=kLoop, calls=%fused_computation.3 | loop fusion | flops 3932160 | bytes 5242880 | tf_op jit(solution)/shard_map/reduce_sum | solution.py:33
  91.5 0.0 copy-done.1
  91.5 0.0 copy-done.2
  91.5 0.0 copy-done.3
  91.5 2.6 %fusion.7 = (bf16[128,2048]{1,0:T(8,128)(2,1)}, f32[128,2048]{1,0:T(8,128)}, f32[128,2048]{1,0:T(8,128)}, bf16[128,2048]{1,0:T(8,128)(2,1)}) fusion(f32[128,2048]{1,0:T(8,128)S(1)} %copy-done.1, f32[128,2048]{1,0:T(8,128)S(1)} %convert_reduce_fusion, f32[]{:T(128)} %bitcast.3, bf16[128,2048]{1,0:T(8,128)(2,1)S(1)} %copy-done.3, f32[128,2048]{1,0:T(8,128)S(1)} %copy-done.2), kind=kLoop, calls=%fused_computation.26 | loop fusion | flops 4194304 | bytes 6815748 | tf_op jit(solution)/shard_map/convert_element_type | solution.py:41
  94.1 0.0 all-gather.2.cloned.1.call-update
  94.1 0.0 reduce-scatter.2.cloned.1.call-start
  94.1 12.1 %fusion = f32[1536,1024]{1,0:T(8,128)} fusion(bf16[1024,2048]{1,0:T(8,128)(2,1)} %param.13, bf16[1536,2048]{1,0:T(8,128)(2,1)} %param.11, pred[1536]{0:T(1024)(128)(4,1)S(1)} %iota_compare_fusion), kind=kOutput, calls=%fused_computation.8 | convolution fusion | flops 6445596672 | bytes 16778752 | tf_op jit(solution)/shard_map/dot_general | solution.py:46
  106.2 0.0 reduce-scatter.2.cloned.1.call-update
  106.3 0.6 scatter_custom_fusion
  106.9 23.3 %all-gather.2.cloned.1.call-done = bf16[1024,2048]{1,0:T(8,128)(2,1)} async-done(((bf16[128,2048]{1,0:T(8,128)(2,1)}), bf16[1024,2048]{1,0:T(8,128)(2,1)}) %all-gather.2.cloned.1.call-update) | async-done | bytes 4194320 | tf_op jit(solution)/shard_map/all_gather | solution.py:41
  130.2 5.0 %gather_fusion.1 = bf16[8,128,2048]{2,1,0:T(8,128)(2,1)} fusion(bf16[8,128,2048]{2,1,0:T(8,128)(2,1)} %bitcast.11, s32[1024]{0:T(1024)S(1)} %pad_clamp_fusion), kind=kCustom, calls=%fused_computation.1.clone | custom fusion | bytes 8388640 | tf_op jit(solution)/shard_map/jit(_take)/gather | solution.py:43
  135.2 4.7 %broadcast_select_fusion.1 = bf16[8,128,2048]{2,1,0:T(8,128)(2,1)} fusion(bf16[8,128,2048]{2,1,0:T(8,128)(2,1)} %gather_fusion.1, pred[8]{0:T(512)(128)(4,1)S(1)} %compare_and_fusion), kind=kLoop, calls=%fused_computation.5 | loop fusion | flops 2097152 | bytes 8388616 | tf_op jit(solution)/shard_map/jit(_take)/select_n | solution.py:43
  139.9 76.9 %reduce-scatter.2.cloned.1.call-done = f32[1536,256]{1,0:T(8,128)} async-done(((f32[1536,1024]{1,0:T(8,128)}), f32[1536,256]{1,0:T(8,128)}) %reduce-scatter.2.cloned.1.call-update) | async-done | bytes 1572880 | tf_op jit(solution)/shard_map/reduce_scatter | solution.py:49
  216.8 2.4 %convert_element_type.35 = bf16[1536,256]{1,0:T(8,128)(2,1)} convert(f32[1536,256]{1,0:T(8,128)} %reduce-scatter.2.cloned.1.call-done) | non-fusion elementwise | flops 393216 | bytes 2359296 | tf_op jit(solution)/shard_map/convert_element_type | solution.py:49
  (6 shorter events, 0.0 us)
Async XLA Ops:
  8.0 2.3 %copy-start = (bf16[1536,1024]{1,0:T(8,128)(2,1)S(1)}, bf16[1536,1024]{1,0:T(8,128)(2,1)}, u32[]{:S(2)}) copy-start(bf16[1536,1024]{1,0:T(8,128)(2,1)} %param.10) | copy-start | bytes 9437188
  31.3 57.0 %all-to-all-start = ((bf16[8,128,2048]{2,1,0:T(8,128)(2,1)}), bf16[8,128,2048]{2,1,0:T(8,128)(2,1)}, u32[]{:S(2)}, u32[]{:S(2)}) async-start(bf16[8,128,2048]{2,1,0:T(8,128)(2,1)} %broadcast_select_fusion.2), calls=%async_computation | async-start | bytes 8388608 | tf_op jit(solution)/shard_map/all_to_all | solution.py:32
  35.8 94.4 %all-gather.2.cloned.1.call-start = ((), (), s32[]{:S(2)}) async-start(), calls=%async_computation.2 | async-start | bytes 4718592 | tf_op jit(solution)/shard_map/all_gather | solution.py:41
  88.3 3.2 %copy-start.1 = (f32[128,2048]{1,0:T(8,128)S(1)}, f32[128,2048]{1,0:T(8,128)}, u32[]{:S(2)}) copy-start(f32[128,2048]{1,0:T(8,128)} %param.15) | copy-start | bytes 3145732
  88.3 3.2 %copy-start.2 = (f32[128,2048]{1,0:T(8,128)S(1)}, f32[128,2048]{1,0:T(8,128)}, u32[]{:S(2)}) copy-start(f32[128,2048]{1,0:T(8,128)} %param.16) | copy-start | bytes 3145732
  88.3 3.2 %copy-start.3 = (bf16[128,2048]{1,0:T(8,128)(2,1)S(1)}, bf16[128,2048]{1,0:T(8,128)(2,1)}, u32[]{:S(2)}) copy-start(bf16[128,2048]{1,0:T(8,128)(2,1)} %param.17) | copy-start | bytes 1572868
  94.1 122.7 %reduce-scatter.2.cloned.1.call-start = ((), (), s32[]{:S(2)}) async-start(), calls=%async_computation.3 | async-start | bytes 7864320 | tf_op jit(solution)/shard_map/reduce_scatter | solution.py:49
Sparse Core Ops, SparseCore 0:
  94.2 35.9 all-gather.1
Sparse Core Ops, SparseCore 1:
  106.3 110.4 reduce-scatter.1
where the time goes:
time: 228 us; the launch traced here: 227 us
  waiting for transfers between devices  100 us (44%)
  blocking collectives  51.7 us (23%)
  matrix products  23.4 us (10%)
  other arithmetic  19.1 us (8%)
  between operations  16.9 us (7%)
  local copies, waits for them, and re-layouts  10.6 us (5%)
  starting transfers between devices  4.63 us (2%)
    reduce_scatter x1, waiting for transfers between devices, per_device(): lax.psum_scatter(feature_part, 'mp', scatter_dimension=1, tiled=True)  76.9 us
    psum x1, blocking collectives, per_device(): total = lax.psum(token_counts, 'dp')  51.7 us
    all_gather x1, waiting for transfers between devices, per_device(): lax.all_gather(master_new.astype(jnp.bfloat16), 'dp', axis=0, tiled=True)  23.3 us
    dot_general x1, matrix products, per_device(): lax.dot_general(masked, down_weight, (((1,), (1,)), ((), ())), preferred_...  12.1 us
    dot_general x1, matrix products, per_device(): lax.dot_general(hidden_acts, masked, (((0,), (0,)), ((), ())), preferred_...  11.4 us
    select_n x2, other arithmetic, per_device(): jnp.take(partial_value.astype(jnp.bfloat16).reshape(workers, block, colum...  5.47 us
    gather x1, local copies, waits for them, and re-layouts, per_device(): jnp.take(gathered.reshape(workers, block, columns), inverse, axis=0)  5.01 us
    gather x1, local copies, waits for them, and re-layouts, per_device(): jnp.take(partial_value.astype(jnp.bfloat16).reshape(workers, block, colum...  4.93 us
  transfers between devices with their start and end apart: 3, of which 2 were waited for; matrix products, arithmetic and copies ran while one was open for 10% of the time, Pallas kernels for 0%

commit v1 on v0

v1 whole, which is shorter than its diff:
```python
import functools

import jax
import jax.numpy as jnp
from jax import lax
from jax.experimental import pallas as pl
from jax.experimental.pallas import tpu as pltpu
from jax.sharding import PartitionSpec as P

beta_one = 0.9
beta_two = 0.95
learn_rate = 0.0003
epsilon = 1e-08
correct_one = 1.0 - 0.9**50
correct_two = 1.0 - 0.95**50

MESH = pl.DeviceIdType.MESH
F32 = jnp.float32
BF16 = jnp.bfloat16
ROW_CHUNKS = 4
COL_CHUNKS = 4


def kernel(
    chips, depth,
    acts_hbm, grads_hbm, count_smem, weight_hbm, owner_smem, master_hbm, moment1_hbm, moment2_hbm,
    master_out, moment1_out, moment2_out, weights_out, input_out,
    acts, acts_t, grads, weight, master, moment1, moment2,
    pick, part, from_mate, to_chip, from_chip, own_sum,
    gathered, z_send, z_recv, z_own, z_out,
    count_tile, count_mate, count_pair, count_chip,
    load_sem, grads_sem, out_sem,
    mate_send, mate_recv, chip_send, chip_recv,
    spread_send, spread_recv, relay_send, relay_recv,
    zs_sem, zr_sem, count_send, count_recv,
):
    rows, columns = grads.shape
    hidden = acts.shape[1]
    slots = 2 * chips
    block = hidden // slots
    share = hidden // depth
    rc = rows // ROW_CHUNKS
    cc = columns // COL_CHUNKS
    tile = 256

    me = lax.axis_index("dp")
    z = lax.axis_index("mp")
    core = lax.rem(me, 2)
    chip = me // 2
    mate = me + 1 - 2 * core
    mate_id = (mate, z)

    def chip_id(k):
        return (2 * lax.rem(chip + k, chips) + core, z)

    def z_id(k):
        return (me, lax.rem(z + k, depth))

    def grads_copy(r):
        span = pl.ds(pl.multiple_of(r * rc, rc), rc)
        return pltpu.make_async_copy(grads_hbm.at[span], grads.at[span], grads_sem.at[r])

    for r in range(ROW_CHUNKS):
        grads_copy(r).start()
    loads = [
        pltpu.make_async_copy(source, target, load_sem.at[i])
        for i, (source, target) in enumerate(
            [
                (weight_hbm, weight),
                (acts_hbm, acts),
                (master_hbm, master),
                (moment1_hbm, moment1),
                (moment2_hbm, moment2),
            ]
        )
    ]
    for copy in loads:
        copy.start()

    barrier = pltpu.get_barrier_semaphore()
    pl.semaphore_signal(barrier, inc=1, device_id=mate_id, device_id_type=MESH)

    @pl.loop(1, chips)
    def _(k):
        pl.semaphore_signal(barrier, inc=1, device_id=chip_id(k), device_id_type=MESH)

    for k in range(1, depth):
        pl.semaphore_signal(barrier, inc=1, device_id=z_id(k), device_id_type=MESH)
    pl.semaphore_wait(barrier, 1 + (chips - 1) + (depth - 1))

    count = count_smem[0]
    count_tile[...] = jnp.full(count_tile.shape, count, jnp.int32)

    def count_mate_copy():
        return pltpu.make_async_remote_copy(
            count_tile, count_mate, count_send.at[0], count_recv.at[0], mate_id, MESH
        )

    def count_chip_copy(k):
        return pltpu.make_async_remote_copy(
            count_pair, count_chip.at[k], count_send.at[k], count_recv.at[k], chip_id(k), MESH
        )

    count_mate_copy().start()

    def feature(r, target):
        span = pl.ds(pl.multiple_of(r * rc, rc), rc)
        value = lax.dot_general(
            grads[span, :],
            weight[pl.ds(pl.multiple_of(target * share, share), share), :],
            (((1,), (1,)), ((), ())),
            preferred_element_type=F32,
        )
        position = lax.broadcasted_iota(jnp.int32, value.shape, 0) + r * rc
        return span, jnp.where(position < count, value, 0.0)

    def z_copy(k, r):
        span = pl.ds(pl.multiple_of(r * rc, rc), rc)
        return pltpu.make_async_remote_copy(
            z_send.at[k - 1, span], z_recv.at[k - 1, span],
            zs_sem.at[k - 1, r], zr_sem.at[k - 1, r], z_id(k), MESH,
        )

    def feature_block(k, first):
        @pl.loop(0, ROW_CHUNKS)
        def _(r):
            if first:
                grads_copy(r).wait()
            span, value = feature(r, lax.rem(z + k, depth))
            z_send[k - 1, span, :] = value.astype(BF16)
            z_copy(k, r).start()

    order = [(depth // 2 + i) % depth for i in range(depth)]
    order = [k for k in order if k]
    loads[0].wait()
    feature_block(order[0], True)

    count_mate_copy().wait_recv()
    count_pair[...] = count_tile[...] + count_mate[...]

    @pl.loop(1, chips)
    def _(k):
        count_chip_copy(k).start()

    loads[1].wait()

    @pl.loop(0, slots)
    def _(j):
        span = pl.ds(pl.multiple_of(j * block, block), block)
        first = owner_smem[j] * block
        unit = lax.broadcasted_iota(jnp.int32, (block, hidden), 1)
        row = lax.broadcasted_iota(jnp.int32, (block, hidden), 0)
        pick[span, :] = jnp.where(unit == row + first, 1.0, 0.0).astype(BF16)

    @pl.loop(0, hidden // tile)
    def _(i):
        span = pl.ds(pl.multiple_of(i * tile, tile), tile)
        turned = lax.dot_general(
            pick[span, :], acts[...], (((1,), (1,)), ((), ())), preferred_element_type=F32
        )
        position = lax.broadcasted_iota(jnp.int32, turned.shape, 1)
        acts_t[span, :] = jnp.where(position < count, turned, 0.0).astype(BF16)

    def mate_copy(q):
        return pltpu.make_async_remote_copy(
            part.at[q, :, 1 - core], from_mate.at[q], mate_send.at[q], mate_recv.at[q],
            mate_id, MESH,
        )

    def chip_copy(q, k):
        return pltpu.make_async_remote_copy(
            to_chip.at[q, k], from_chip.at[q, k], chip_send.at[q, k], chip_recv.at[q, k],
            chip_id(k), MESH,
        )

    pairs = tile // (2 * block)

    def partial_chunk(q):
        across = pl.ds(pl.multiple_of(q * cc, cc), cc)

        @pl.loop(0, hidden // tile)
        def _(i):
            span = pl.ds(pl.multiple_of(i * tile, tile), tile)
            value = jnp.dot(acts_t[span, :], grads[:, across], preferred_element_type=F32)
            part[q, pl.ds(i * pairs, pairs)] = value.astype(BF16).reshape(pairs, 2, block, cc)

        mate_copy(q).start()

    def pair_chunk(q):
        mate_copy(q).wait_recv()

        @pl.loop(1, chips)
        def _(k):
            there = lax.rem(chip + k, chips)
            both = part[q, there, core].astype(F32) + from_mate[q, there].astype(F32)
            to_chip[q, k] = both.astype(BF16)
            chip_copy(q, k).start()

        own_sum[q] = part[q, chip, core].astype(F32) + from_mate[q, chip].astype(F32)

    partial_chunk(0)

    @pl.loop(1, COL_CHUNKS)
    def _(q):
        partial_chunk(q)
        pair_chunk(q - 1)

    pair_chunk(COL_CHUNKS - 1)

    for k in order[1:]:
        feature_block(k, False)

    @pl.loop(0, ROW_CHUNKS)
    def _(r):
        span, value = feature(r, z)
        z_own[span, :] = value

    @pl.loop(1, chips)
    def _(k):
        count_chip_copy(k).wait_recv()

    total = lax.fori_loop(1, chips, lambda k, t: t + count_chip[k], count_pair[...])
    total = total[0:1, 0:1].astype(F32)
    for copy in loads[2:]:
        copy.wait()

    def spread_copy(q, k):
        across = pl.ds(pl.multiple_of(q * cc, cc), cc)
        return pltpu.make_async_remote_copy(
            gathered.at[me, :, across], gathered.at[me, :, across],
            spread_send.at[q, k], spread_recv.at[q, k], chip_id(k), MESH,
        )

    def relay_copy(q, k):
        slot = 2 * lax.rem(chip + chips - k, chips) + core
        across = pl.ds(pl.multiple_of(q * cc, cc), cc)
        return pltpu.make_async_remote_copy(
            gathered.at[slot, :, across], gathered.at[slot, :, across],
            relay_send.at[q, k], relay_recv.at[q, k], mate_id, MESH,
        )

    @pl.loop(0, COL_CHUNKS)
    def _(q):
        across = pl.ds(pl.multiple_of(q * cc, cc), cc)

        @pl.loop(1, chips)
        def _(k):
            chip_copy(q, k).wait_recv()
            own_sum[q] = own_sum[q] + from_chip[q, k].astype(F32)

        grad = own_sum[q] / total
        moment1_new = beta_one * moment1[:, across] + (1.0 - beta_one) * grad
        second = beta_two * moment2[:, across].astype(F32) + (1.0 - beta_two) * grad * grad
        moment1[:, across] = moment1_new
        moment2[:, across] = second.astype(BF16)
        master_new = master[:, across] - learn_rate * (moment1_new / correct_one) / (
            jnp.sqrt(second / correct_two) + epsilon
        )
        master[:, across] = master_new
        gathered[me, :, across] = master_new.astype(BF16)

        @pl.loop(1, chips)
        def _(k):
            spread_copy(q, k).start()

        relay_copy(q, 0).start()

    stores = [
        pltpu.make_async_copy(source, target, out_sem.at[i])
        for i, (source, target) in enumerate(
            [
                (master, master_out),
                (moment1, moment1_out),
                (moment2, moment2_out),
                (gathered, weights_out),
                (z_out, input_out),
            ]
        )
    ]
    for copy in stores[:3]:
        copy.start()

    @pl.loop(0, COL_CHUNKS)
    def _(q):
        @pl.loop(1, chips)
        def _(k):
            spread_copy(q, k).wait_recv()
            relay_copy(q, k).start()

    @pl.loop(0, COL_CHUNKS)
    def _(q):
        @pl.loop(0, chips)
        def _(k):
            relay_copy(q, k).wait_recv()

    stores[3].start()

    @pl.loop(0, ROW_CHUNKS)
    def _(r):
        span = pl.ds(pl.multiple_of(r * rc, rc), rc)
        value = z_own[span, :]
        for k in range(1, depth):
            z_copy(k, r).wait_recv()
            value = value + z_recv[k - 1, span, :].astype(F32)
        z_out[span, :] = value.astype(BF16)

    stores[4].start()

    count_mate_copy().wait_send()

    @pl.loop(1, chips)
    def _(k):
        count_chip_copy(k).wait_send()

    @pl.loop(0, COL_CHUNKS)
    def _(q):
        mate_copy(q).wait_send()
        relay_copy(q, 0).wait_send()

        @pl.loop(1, chips)
        def _(k):
            chip_copy(q, k).wait_send()
            spread_copy(q, k).wait_send()
            relay_copy(q, k).wait_send()

    @pl.loop(0, ROW_CHUNKS)
    def _(r):
        for k in range(1, depth):
            z_copy(k, r).wait_send()

    for copy in stores:
        copy.wait()


def place_kernel(owner_smem, *refs):
    arrays, sem = refs[:-1], refs[-1]
    count = len(arrays) // 2
    slots = arrays[3].shape[0]
    copies = [
        pltpu.make_async_copy(arrays[3].at[j], arrays[count + 3].at[owner_smem[j]], sem.at[j])
        for j in range(slots)
    ]
    copies += [
        pltpu.make_async_copy(arrays[i], arrays[count + i], sem.at[slots + i])
        for i in range(count)
        if i != 3
    ]
    for copy in copies:
        copy.start()
    for copy in copies:
        copy.wait()


def place(owner_map, results):
    slots, block, columns = results[3].shape
    hbm = pl.BlockSpec(memory_space=pl.ANY)
    outs = pl.pallas_call(
        place_kernel,
        out_shape=tuple(jax.ShapeDtypeStruct(x.shape, x.dtype) for x in results),
        in_specs=[pl.BlockSpec(memory_space=pltpu.SMEM)] + [hbm] * len(results),
        out_specs=(hbm,) * len(results),
        scratch_shapes=[pltpu.SemaphoreType.DMA((slots + len(results),))],
    )(owner_map, *results)
    return (*outs[:3], outs[3].reshape(slots * block, columns), outs[4])


def per_device(
    hidden_acts, out_grads, token_counts, down_weight, owner_map, master, moment1, moment2
):
    rows, columns = out_grads.shape
    hidden = hidden_acts.shape[1]
    slots = lax.axis_size("dp")
    depth = lax.axis_size("mp")
    chips = slots // 2
    block = hidden // slots
    share = hidden // depth
    cc = columns // COL_CHUNKS
    smem = pl.BlockSpec(memory_space=pltpu.SMEM)
    hbm = pl.BlockSpec(memory_space=pl.ANY)
    vmem = pltpu.VMEM
    dma = pltpu.SemaphoreType.DMA
    pieces = (COL_CHUNKS, chips, block, cc)
    results = pl.pallas_call(
        functools.partial(kernel, chips, depth),
        out_shape=(
            jax.ShapeDtypeStruct(master.shape, F32),
            jax.ShapeDtypeStruct(moment1.shape, F32),
            jax.ShapeDtypeStruct(moment2.shape, BF16),
            jax.ShapeDtypeStruct((slots, block, columns), BF16),
            jax.ShapeDtypeStruct((rows, share), BF16),
        ),
        in_specs=[hbm, hbm, smem, hbm, smem, hbm, hbm, hbm],
        out_specs=(hbm,) * 5,
        scratch_shapes=[
            vmem(hidden_acts.shape, BF16),
            vmem((hidden, rows), BF16),
            vmem((rows, columns), BF16),
            vmem((hidden, columns), BF16),
            vmem(master.shape, F32),
            vmem(moment1.shape, F32),
            vmem(moment2.shape, BF16),
            vmem((hidden, hidden), BF16),
            vmem((COL_CHUNKS, chips, 2, block, cc), BF16),
            vmem(pieces, BF16),
            vmem(pieces, BF16),
            vmem(pieces, BF16),
            vmem((COL_CHUNKS, block, cc), F32),
            vmem((slots, block, columns), BF16),
            vmem((depth - 1, rows, share), BF16),
            vmem((depth - 1, rows, share), BF16),
            vmem((rows, share), F32),
            vmem((rows, share), BF16),
            vmem((8, 128), jnp.int32),
            vmem((8, 128), jnp.int32),
            vmem((8, 128), jnp.int32),
            vmem((chips, 8, 128), jnp.int32),
            dma((5,)),
            dma((ROW_CHUNKS,)),
            dma((5,)),
            dma((COL_CHUNKS,)),
            dma((COL_CHUNKS,)),
            dma((COL_CHUNKS, chips)),
            dma((COL_CHUNKS, chips)),
            dma((COL_CHUNKS, chips)),
            dma((COL_CHUNKS, chips)),
            dma((COL_CHUNKS, chips)),
            dma((COL_CHUNKS, chips)),
            dma((depth - 1, ROW_CHUNKS)),
            dma((depth - 1, ROW_CHUNKS)),
            dma((chips,)),
            dma((chips,)),
        ],
        compiler_params=pltpu.CompilerParams(
            collective_id=0, has_side_effects=True, vmem_limit_bytes=60 * 1024 * 1024
        ),
        cost_estimate=pl.CostEstimate(
            flops=4 * rows * columns * hidden,
            bytes_accessed=2 * (rows * hidden + rows * columns + 2 * hidden * columns),
            transcendentals=0,
        ),
    )(hidden_acts, out_grads, token_counts, down_weight, owner_map, master, moment1, moment2)
    return place(owner_map, results)


def solution(mesh):
    in_specs = (
        P("dp", None),
        P("dp", "mp"),
        P("dp"),
        P(None, "mp"),
        P(),
        P("dp", "mp"),
        P("dp", "mp"),
        P("dp", "mp"),
    )
    out_specs = (P("dp", "mp"), P("dp", "mp"), P("dp", "mp"), P(None, "mp"), P("dp", "mp"))
    return jax.shard_map(
        per_device, mesh=mesh, in_specs=in_specs, out_specs=out_specs, check_vma=False
    )
```

time: 228 us -> 312 us (1.37)
  Pallas kernels: 0 us -> 307 us
  waiting for transfers between devices: 100 us -> 0 us
  blocking collectives: 51.7 us -> 0 us
  matrix products: 23.4 us -> 0 us
  other arithmetic: 19.1 us -> 0 us
  between operations: 16.9 us -> 1.29 us
  local copies, waits for them, and re-layouts: 10.6 us -> 0 us
  starting transfers between devices: 4.63 us -> 0 us
    pallas_call x0 -> x2, Pallas kernels: none -> 307 us  [the longest x1 232 us: place(): pl.pallas_call(place_kernel, out_shape=tuple((jax.ShapeDtypeStruct(x.shap...]
    reduce_scatter x1 -> x0, waiting for transfers between devices: 76.9 us -> none  [per_device(): lax.psum_scatter(feature_part, 'mp', scatter_dimension=1, tiled=True)]
    psum x1 -> x0, blocking collectives: 51.7 us -> none  [per_device(): total = lax.psum(token_counts, 'dp')]
    dot_general x2 -> x0, matrix products: 23.4 us -> none  [the longest x1 12.1 us: per_device(): lax.dot_general(masked, down_weight, (((1,), (1,)), ((), ())), preferred_...]
    all_gather x1 -> x0, waiting for transfers between devices: 23.3 us -> none  [per_device(): lax.all_gather(master_new.astype(jnp.bfloat16), 'dp', axis=0, tiled=True)]
    select_n x4 -> x0, other arithmetic: 10.1 us -> none  [the longest x2 5.47 us: per_device(): jnp.take(partial_value.astype(jnp.bfloat16).reshape(workers, block, colum...]
    gather x2 -> x0, local copies, waits for them, and re-layouts: 9.95 us -> none  [the longest x1 5.01 us: per_device(): jnp.take(gathered.reshape(workers, block, columns), inverse, axis=0)]
    convert_element_type x2 -> x0, other arithmetic: 4.93 us -> none  [the longest x1 2.57 us: per_device(): master_new.astype(jnp.bfloat16)]
  transfers between devices with their start and end apart: 3 -> 0, of which waited for: 2 -> 0; matrix products, arithmetic and copies ran while one was open for 10% -> 0% of each run, Pallas kernels for 0% -> 0%
where the time goes in v1:
time: 312 us; the launch traced here: 308 us
  Pallas kernels  307 us (98%)
    pallas_call x1, Pallas kernels, place(): pl.pallas_call(place_kernel, out_shape=tuple((jax.ShapeDtypeStruct(x.shap...  232 us
    pallas_call x1, Pallas kernels, per_device(): pl.pallas_call(functools.partial(kernel, chips, depth), out_shape=(jax.Sh...  74.9 us

profile of v1, /device:TPU:16, one launch (start us, length us, event | category | flops | bytes accessed | tf_op | source)
XLA Modules:
  0.0 308.4 jit_solution(5108191355273226580)
XLA Ops:
  1.3 74.9 %shard_map.119 = (f32[128,2048]{1,0:T(8,128)}, f32[128,2048]{1,0:T(8,128)}, bf16[128,2048]{1,0:T(8,128)(2,1)}, bf16[8,128,2048]{2,1,0:T(8,128)(2,1)}, bf16[1536,256]{1,0:T(8,128)(2,1)}) custom-call(bf16[1536,1024]{1,0:T(8,128)(2,1)} %acts_hbm.1, bf16[1536,2048]{1,0:T(8,128)(2,1)} %grads_hbm.1, s32[1]{0:T(128)S(6)} %copy.13.count_smem, ...), custom_call_target="tpu_custom_call" | custom-call | flops 12884901888 | bytes 17825792 | tf_op jit(solution)/shard_map/pallas_call | solution.py:383
  76.2 232.2 %shard_map.120 = (f32[128,2048]{1,0:T(8,128)}, f32[128,2048]{1,0:T(8,128)}, bf16[128,2048]{1,0:T(8,128)(2,1)}, bf16[8,128,2048]{2,1,0:T(8,128)(2,1)}, bf16[1536,256]{1,0:T(8,128)(2,1)}) custom-call(s32[8]{0:T(128)} %owner_smem.3, f32[128,2048]{1,0:T(8,128)} %get-tuple-element.15.refs_0_, f32[128,2048]{1,0:T(8,128)} %get-tuple-element.16.refs_1_, ...), custom_call_target="tpu_custom_call" | custom-call | tf_op jit(solution)/shard_map/pallas_call | solution.py:357

commit v2 on v1

--- a/solution.py
+++ b/solution.py
@@ -27,12 +27,12 @@
     master_out, moment1_out, moment2_out, weights_out, input_out,
     acts, acts_t, grads, weight, master, moment1, moment2,
     pick, part, from_mate, to_chip, from_chip, own_sum,
-    gathered, z_send, z_recv, z_own, z_out,
+    gathered, z_half, z_in, z_part, z_full, z_out,
     count_tile, count_mate, count_pair, count_chip,
     load_sem, grads_sem, out_sem,
     mate_send, mate_recv, chip_send, chip_recv,
     spread_send, spread_recv, relay_send, relay_recv,
-    zs_sem, zr_sem, count_send, count_recv,
+    half_send, half_recv, full_send, full_recv, count_send, count_recv,
 ):
     rows, columns = grads.shape
     hidden = acts.shape[1]
@@ -114,26 +114,90 @@
         position = lax.broadcasted_iota(jnp.int32, value.shape, 0) + r * rc
         return span, jnp.where(position < count, value, 0.0)
 
-    def z_copy(k, r):
+    def aim(way, c):
+        target = depth - 1 - c if way == 0 else c
+        taking = z < target if way == 0 else z > target
+        hop = z if way == 0 else depth - 1 - z
+        neighbour = (me, z + 1 if way == 0 else z - 1)
+        return target, taking, hop, neighbour
+
+    def half_copy(way, c, r):
         span = pl.ds(pl.multiple_of(r * rc, rc), rc)
-        return pltpu.make_async_remote_copy(
-            z_send.at[k - 1, span], z_recv.at[k - 1, span],
-            zs_sem.at[k - 1, r], zr_sem.at[k - 1, r], z_id(k), MESH,
-        )
-
-    def feature_block(k, first):
-        @pl.loop(0, ROW_CHUNKS)
-        def _(r):
-            if first:
-                grads_copy(r).wait()
-            span, value = feature(r, lax.rem(z + k, depth))
-            z_send[k - 1, span, :] = value.astype(BF16)
-            z_copy(k, r).start()
-
-    order = [(depth // 2 + i) % depth for i in range(depth)]
-    order = [k for k in order if k]
+        target, _, _, neighbour = aim(way, c)
+        return pltpu.make_async_remote_copy(
+            z_half.at[target, span], z_in.at[way, c, span],
+            half_send.at[way, c, r], half_recv.at[way, c, r], neighbour, MESH,
+        )
+
+    def full_copy(way, r):
+        span = pl.ds(pl.multiple_of(r * rc, rc), rc)
+        target, _, _, neighbour = aim(way, 0)
+        return pltpu.make_async_remote_copy(
+            z_part.at[target, span], z_full.at[way, span],
+            full_send.at[way, r], full_recv.at[way, r], neighbour, MESH,
+        )
+
+    def feature_block(way, c):
+        target, taking, hop, _ = aim(way, c)
+
+        @pl.when(taking)
+        def _():
+            @pl.loop(0, ROW_CHUNKS)
+            def _(r):
+                if c == 0:
+
+                    @pl.when(z < depth - 1 if way == 0 else z == depth - 1)
+                    def _():
+                        grads_copy(r).wait()
+
+                span, value = feature(r, target)
+
+                @pl.when(hop == 0)
+                def _():
+                    z_half[target, span, :] = value.astype(BF16)
+                    half_copy(way, c, r).start()
+
+                @pl.when(hop > 0)
+                def _():
+                    z_part[target, span, :] = value
+
+    def forward(c, step):
+        for way in range(2):
+            target, taking, hop, _ = aim(way, c)
+            r = step - hop
+
+            @pl.when(taking & (hop > 0) & (r >= 0) & (r < ROW_CHUNKS))
+            def _():
+                span = pl.ds(pl.multiple_of(r * rc, rc), rc)
+                if c > 0:
+                    half_copy(way, c, r).wait_recv()
+                    value = z_part[target, span, :] + z_in[way, c, span, :].astype(F32)
+                    z_half[target, span, :] = value.astype(BF16)
+                    half_copy(way, c, r).start()
+                else:
+
+                    @pl.when(hop == 1)
+                    def _():
+                        half_copy(way, c, r).wait_recv()
+                        z_part[target, span, :] += z_in[way, c, span, :].astype(F32)
+
+                    @pl.when(hop > 1)
+                    def _():
+                        full_copy(way, r).wait_recv()
+                        z_part[target, span, :] += z_full[way, span, :]
+
+                    full_copy(way, r).start()
+
+    last_step = ROW_CHUNKS + depth - 3
+    forwards = [(c, step) for c in range(depth - 2) for step in range(1, last_step + 1)]
+
+    def forward_some(count):
+        for _ in range(min(count, len(forwards))):
+            forward(*forwards.pop(0))
+
     loads[0].wait()
-    feature_block(order[0], True)
+    feature_block(0, 0)
+    feature_block(1, 0)
 
     count_mate_copy().wait_recv()
     count_pair[...] = count_tile[...] + count_mate[...]
@@ -198,22 +262,25 @@
 
         own_sum[q] = part[q, chip, core].astype(F32) + from_mate[q, chip].astype(F32)
 
-    partial_chunk(0)
-
-    @pl.loop(1, COL_CHUNKS)
-    def _(q):
+    forward_some(1)
+    for q in range(COL_CHUNKS):
         partial_chunk(q)
-        pair_chunk(q - 1)
-
+        if q > 0:
+            pair_chunk(q - 1)
+        if q == COL_CHUNKS // 2:
+            forward_some(1)
     pair_chunk(COL_CHUNKS - 1)
 
-    for k in order[1:]:
-        feature_block(k, False)
+    for c in range(1, depth - 1):
+        feature_block(0, c)
+        feature_block(1, c)
+        if c == 1:
+            forward_some(1)
 
     @pl.loop(0, ROW_CHUNKS)
     def _(r):
         span, value = feature(r, z)
-        z_own[span, :] = value
+        z_part[z, span, :] = value
 
     @pl.loop(1, chips)
     def _(k):
@@ -239,8 +306,7 @@
             relay_send.at[q, k], relay_recv.at[q, k], mate_id, MESH,
         )
 
-    @pl.loop(0, COL_CHUNKS)
-    def _(q):
+    def update_chunk(q):
         across = pl.ds(pl.multiple_of(q * cc, cc), cc)
 
         @pl.loop(1, chips)
@@ -264,6 +330,11 @@
             spread_copy(q, k).start()
 
         relay_copy(q, 0).start()
+
+    for q in range(COL_CHUNKS):
+        update_chunk(q)
+        if q > 0:
+            forward_some(1)
 
     stores = [
         pltpu.make_async_copy(source, target, out_sem.at[i])
@@ -280,6 +351,8 @@
     for copy in stores[:3]:
         copy.start()
 
+    forward_some(len(forwards))
+
     @pl.loop(0, COL_CHUNKS)
     def _(q):
         @pl.loop(1, chips)
@@ -298,11 +371,22 @@
     @pl.loop(0, ROW_CHUNKS)
     def _(r):
         span = pl.ds(pl.multiple_of(r * rc, rc), rc)
-        value = z_own[span, :]
-        for k in range(1, depth):
-            z_copy(k, r).wait_recv()
-            value = value + z_recv[k - 1, span, :].astype(F32)
-        z_out[span, :] = value.astype(BF16)
+        for way in range(2):
+            hop = z if way == 0 else depth - 1 - z
+            c = depth - 1 - hop
+            wide = (hop == depth - 1) & (depth > 2)
+
+            @pl.when((hop > 0) & wide)
+            def _():
+                full_copy(way, r).wait_recv()
+                z_part[z, span, :] += z_full[way, span, :]
+
+            @pl.when((hop > 0) & jnp.logical_not(wide))
+            def _():
+                half_copy(way, c, r).wait_recv()
+                z_part[z, span, :] += z_in[way, c, span, :].astype(F32)
+
+        z_out[span, :] = z_part[z, span, :].astype(BF16)
 
     stores[4].start()
 
@@ -325,41 +409,56 @@
 
     @pl.loop(0, ROW_CHUNKS)
     def _(r):
-        for k in range(1, depth):
-            z_copy(k, r).wait_send()
+        for way in range(2):
+            for c in range(depth - 1):
+                _, taking, hop, _ = aim(way, c)
+
+                @pl.when(taking & (hop == 0) if c == 0 else taking)
+                def _():
+                    half_copy(way, c, r).wait_send()
+
+            _, taking, hop, _ = aim(way, 0)
+
+            @pl.when(taking & (hop > 0))
+            def _():
+                full_copy(way, r).wait_send()
 
     for copy in stores:
         copy.wait()
 
 
 def place_kernel(owner_smem, *refs):
-    arrays, sem = refs[:-1], refs[-1]
-    count = len(arrays) // 2
-    slots = arrays[3].shape[0]
-    copies = [
-        pltpu.make_async_copy(arrays[3].at[j], arrays[count + 3].at[owner_smem[j]], sem.at[j])
-        for j in range(slots)
+    count = len(refs) // 3
+    sources, targets, held = refs[:count], refs[count : 2 * count], refs[2 * count : 3 * count]
+    in_sem, out_sem = refs[3 * count :]
+    slots = held[3].shape[0]
+    moves = [
+        (sources[3].at[j], held[3].at[j], targets[3].at[owner_smem[j]]) for j in range(slots)
     ]
-    copies += [
-        pltpu.make_async_copy(arrays[i], arrays[count + i], sem.at[slots + i])
-        for i in range(count)
-        if i != 3
-    ]
-    for copy in copies:
-        copy.start()
-    for copy in copies:
-        copy.wait()
+    moves += [(sources[i], held[i], targets[i]) for i in range(count) if i != 3]
+    fills = [pltpu.make_async_copy(m[0], m[1], in_sem.at[i]) for i, m in enumerate(moves)]
+    drains = [pltpu.make_async_copy(m[1], m[2], out_sem.at[i]) for i, m in enumerate(moves)]
+    for fill in fills:
+        fill.start()
+    for fill, drain in zip(fills, drains):
+        fill.wait()
+        drain.start()
+    for drain in drains:
+        drain.wait()
 
 
 def place(owner_map, results):
     slots, block, columns = results[3].shape
     hbm = pl.BlockSpec(memory_space=pl.ANY)
+    moves = slots + len(results) - 1
     outs = pl.pallas_call(
         place_kernel,
         out_shape=tuple(jax.ShapeDtypeStruct(x.shape, x.dtype) for x in results),
         in_specs=[pl.BlockSpec(memory_space=pltpu.SMEM)] + [hbm] * len(results),
         out_specs=(hbm,) * len(results),
-        scratch_shapes=[pltpu.SemaphoreType.DMA((slots + len(results),))],
+        scratch_shapes=[pltpu.VMEM(x.shape, x.dtype) for x in results]
+        + [pltpu.SemaphoreType.DMA((moves,)), pltpu.SemaphoreType.DMA((moves,))],
+        compiler_params=pltpu.CompilerParams(vmem_limit_bytes=60 * 1024 * 1024),
     )(owner_map, *results)
     return (*outs[:3], outs[3].reshape(slots * block, columns), outs[4])
 
@@ -406,9 +505,10 @@
             vmem(pieces, BF16),
             vmem((COL_CHUNKS, block, cc), F32),
             vmem((slots, block, columns), BF16),
-            vmem((depth - 1, rows, share), BF16),
-            vmem((depth - 1, rows, share), BF16),
-            vmem((rows, share), F32),
+            vmem((depth, rows, share), BF16),
+            vmem((2, depth - 1, rows, share), BF16),
+            vmem((depth, rows, share), F32),
+            vmem((2, rows, share), F32),
             vmem((rows, share), BF16),
             vmem((8, 128), jnp.int32),
             vmem((8, 128), jnp.int32),
@@ -425,8 +525,10 @@
             dma((COL_CHUNKS, chips)),
             dma((COL_CHUNKS, chips)),
             dma((COL_CHUNKS, chips)),
-            dma((depth - 1, ROW_CHUNKS)),
-            dma((depth - 1, ROW_CHUNKS)),
+            dma((2, depth - 1, ROW_CHUNKS)),
+            dma((2, depth - 1, ROW_CHUNKS)),
+            dma((2, ROW_CHUNKS)),
+            dma((2, ROW_CHUNKS)),
             dma((chips,)),
             dma((chips,)),
         ],

time: 312 us -> 81.5 us (0.26); the launches traced: 308 us -> 81.3 us
  Pallas kernels: 307 us -> 80 us
    pallas_call x1, Pallas kernels: 232 us -> 6.6 us  [place(): pl.pallas_call(place_kernel, out_shape=tuple((jax.ShapeDtypeStruct(x.shap...]
where the time goes in v2:
time: 81.5 us; the launch traced here: 81.3 us
  Pallas kernels  80 us (98%)
  between operations  1.29 us (2%)
    pallas_call x1, Pallas kernels, per_device(): pl.pallas_call(functools.partial(kernel, chips, depth), out_shape=(jax.Sh...  73.4 us
    pallas_call x1, Pallas kernels, place(): pl.pallas_call(place_kernel, out_shape=tuple((jax.ShapeDtypeStruct(x.shap...  6.6 us

profile of v2, /device:TPU:16, one launch (start us, length us, event | category | flops | bytes accessed | tf_op | source)
XLA Modules:
  0.0 81.3 jit_solution(10104193213462011325)
XLA Ops:
  1.3 73.4 %shard_map.119 = (f32[128,2048]{1,0:T(8,128)}, f32[128,2048]{1,0:T(8,128)}, bf16[128,2048]{1,0:T(8,128)(2,1)}, bf16[8,128,2048]{2,1,0:T(8,128)(2,1)}, bf16[1536,256]{1,0:T(8,128)(2,1)}) custom-call(bf16[1536,1024]{1,0:T(8,128)(2,1)} %acts_hbm.1, bf16[1536,2048]{1,0:T(8,128)(2,1)} %grads_hbm.1, s32[1]{0:T(128)S(6)} %copy.13.count_smem, ...), custom_call_target="tpu_custom_call" | custom-call | flops 12884901888 | bytes 17825792 | tf_op jit(solution)/shard_map/pallas_call | solution.py:482
  74.7 6.6 %shard_map.120 = (f32[128,2048]{1,0:T(8,128)}, f32[128,2048]{1,0:T(8,128)}, bf16[128,2048]{1,0:T(8,128)(2,1)}, bf16[8,128,2048]{2,1,0:T(8,128)(2,1)}, bf16[1536,256]{1,0:T(8,128)(2,1)}) custom-call(s32[8]{0:T(128)} %owner_smem.3, f32[128,2048]{1,0:T(8,128)} %get-tuple-element.15.refs_0_, f32[128,2048]{1,0:T(8,128)} %get-tuple-element.16.refs_1_, ...), custom_call_target="tpu_custom_call" | custom-call | tf_op jit(solution)/shard_map/pallas_call | solution.py:454
